TPU v7x, 32 devices: a whole 2x2x4 slice. The times are simulated.
32 devices in a mesh: dp: 2 (over core), seq: 8 (over z, x), tp: 2 (over y).
Axes of the slice: x: 2, y: 2, z: 4, core: 2. Of those that a mesh axis runs over, the one named last changes fastest.
Arguments:
- projected: bfloat16 [4096, 3, 2048], P(('dp', 'seq'), None, 'tp'), may hold values from -24 to 24
- destinations: int32 [4096], P(('dp', 'seq')), may hold values from 0 to 7, as said below
- gather_ids: int32 [4096], P(('dp', 'seq')), may hold values from 0 to 63, as said below
- out_weight: bfloat16 [2048, 2048], P('tp'), may hold values from -0.125 to 0.125
- grad_output: bfloat16 [4096, 2048], P(('dp', 'seq'), 'tp'), may hold values from -6 to 6
Outputs:
- output: bfloat16 [4096, 2048], P(('dp', 'seq'), 'tp')
- grad_projected: bfloat16 [4096, 3, 2048], P(('dp', 'seq'), None, 'tp')
- grad_weight: float32 [2048, 2048], P('tp')
Inputs may be any that keep to these rules, and one draw needn't show every extreme that they name: `destinations`: the 256 rows of one device form runs of 64 consecutive rows that name one sequence rank; the runs of one device name different ranks; in each dp index one rank is named by one run of every device. `gather_ids`: all rows of a run carry one gather number; a row packed into sequence rank r of dp index g carries a number from (g * 8 + r) * 4 to that plus 4 - 1.
All inputs are finite; a program needn't handle non-finite values.
Results may differ from a plain program's by a relative error of at most 0.022.
Values may be sent and summed in bfloat16 or wider, within the bound.
A program may use at most 128 MiB of HBM per device.

v0:
```python
import math

import jax
import jax.numpy as jnp
from jax import lax
from jax.sharding import PartitionSpec as P

HD = 128


masked_score = -1e30


def on_device(projected, destinations, gather_ids, out_weight, grad_output):
    rank_count = lax.axis_size("seq")
    row_count = projected.shape[0]
    run_rows = 2 * row_count // rank_count
    width_local = projected.shape[2]
    head_count = width_local // HD
    run_count = row_count // run_rows
    slot_count = rank_count * run_rows
    scaling = 1.0 / math.sqrt(HD)
    run_target = destinations.reshape(run_count, run_rows)[:, 0]
    run_gather = gather_ids.reshape(run_count, run_rows)[:, 0]
    picked_mask = run_target[None, :] == jnp.arange(rank_count, dtype=jnp.int32)[:, None]
    selector = picked_mask.astype(jnp.bfloat16)

    def pack_rows(values):
        features = values.shape[1]
        blocks = values.reshape(run_count, run_rows * features)
        packed = jnp.dot(selector, blocks, preferred_element_type=jnp.float32)
        return packed.astype(jnp.bfloat16).reshape(rank_count, run_rows, features)

    def unpack_rows(buffer):
        features = buffer.shape[2]
        flat = buffer.reshape(rank_count, run_rows * features)
        rows_back = lax.dot_general(
            selector, flat, (((0,), (0,)), ((), ())), preferred_element_type=jnp.float32
        )
        return rows_back.astype(jnp.bfloat16).reshape(row_count, features)

    slot_gather = jnp.where(
        jnp.any(picked_mask, axis=1),
        jnp.sum(jnp.where(picked_mask, run_gather[None, :], 0), axis=1),
        -1,
    )
    gather_send = jnp.broadcast_to(slot_gather[:, None], (rank_count, run_rows))
    packed_send = pack_rows(projected.reshape(row_count, 3 * width_local))
    received, received_ids = (
        lax.all_to_all(packed_send, "seq", split_axis=0, concat_axis=0, tiled=True),
        lax.all_to_all(gather_send, "seq", split_axis=0, concat_axis=0, tiled=True),
    )
    received = received.reshape(slot_count, 3, width_local)
    key_ids = received_ids.reshape(slot_count)
    matching = key_ids[:, None] == key_ids[None, :]

    def head_inputs(head_index):
        lower = head_index * HD
        return (
            received[:, 0, lower : lower + HD],
            received[:, 1, lower : lower + HD],
            received[:, 2, lower : lower + HD],
        )

    def probabilities(query_head, key_head):
        scores = (
            lax.dot_general(
                query_head, key_head, (((1,), (1,)), ((), ())), preferred_element_type=jnp.float32
            )
            * scaling
        )
        scores = jnp.where(matching, scores, masked_score)
        peak = jnp.max(scores, axis=1, keepdims=True)
        raised = jnp.exp(scores - peak)
        return raised / jnp.sum(raised, axis=1, keepdims=True)

    results = []
    for head_index in range(head_count):
        query_head, key_head, value_head = head_inputs(head_index)
        weights = probabilities(query_head, key_head).astype(jnp.bfloat16)
        results.append(
            jnp.dot(weights, value_head, preferred_element_type=jnp.float32).astype(jnp.bfloat16)
        )
    attended = jnp.concatenate(results, axis=1)
    returned = lax.all_to_all(
        attended.reshape(rank_count, run_rows, width_local),
        "seq",
        split_axis=0,
        concat_axis=0,
        tiled=True,
    )
    attended_rows = unpack_rows(returned)
    partial_terms = jnp.dot(attended_rows, out_weight, preferred_element_type=jnp.float32)
    output = lax.psum_scatter(partial_terms, "tp", scatter_dimension=1, tiled=True).astype(
        jnp.bfloat16
    )
    shard_cols = lax.all_gather(grad_output, "tp", axis=1, tiled=True)
    grad_rows = lax.dot_general(
        shard_cols, out_weight, (((1,), (1,)), ((), ())), preferred_element_type=jnp.float32
    )
    product = lax.dot_general(
        attended_rows, shard_cols, (((0,), (0,)), ((), ())), preferred_element_type=jnp.float32
    )
    grad_block = product
    grad_rows, grad_block = (grad_rows, grad_block)
    row_total = row_count * lax.axis_size("dp") * rank_count
    grad_weight = lax.psum(grad_block, ("dp", "seq")) * (1.0 / math.sqrt(row_total))
    grad_attended = grad_rows.astype(jnp.bfloat16)
    grad_slots = lax.all_to_all(
        pack_rows(grad_attended), "seq", split_axis=0, concat_axis=0, tiled=True
    )
    grad_slots = grad_slots.reshape(slot_count, width_local)
    query_grads = []
    key_grads = []
    value_grads = []
    for head_index in range(head_count):
        query_head, key_head, value_head = head_inputs(head_index)
        lower = head_index * HD
        grad_head = grad_slots[:, lower : lower + HD]
        result_head = attended[:, lower : lower + HD]
        weights = probabilities(query_head, key_head)
        weights_low = weights.astype(jnp.bfloat16)
        grad_weights = lax.dot_general(
            grad_head, value_head, (((1,), (1,)), ((), ())), preferred_element_type=jnp.float32
        )
        delta = jnp.sum(
            grad_head.astype(jnp.float32) * result_head.astype(jnp.float32), axis=1, keepdims=True
        )
        grad_scores = (weights * (grad_weights - delta)).astype(jnp.bfloat16)
        query_grads.append(
            (jnp.dot(grad_scores, key_head, preferred_element_type=jnp.float32) * scaling).astype(
                jnp.bfloat16
            )
        )
        key_grads.append(
            (
                lax.dot_general(
                    grad_scores,
                    query_head,
                    (((0,), (0,)), ((), ())),
                    preferred_element_type=jnp.float32,
                )
                * scaling
            ).astype(jnp.bfloat16)
        )
        value_grads.append(
            lax.dot_general(
                weights_low, grad_head, (((0,), (0,)), ((), ())), preferred_element_type=jnp.float32
            ).astype(jnp.bfloat16)
        )
    stacked = jnp.stack(
        [
            jnp.concatenate(query_grads, axis=1),
            jnp.concatenate(key_grads, axis=1),
            jnp.concatenate(value_grads, axis=1),
        ],
        axis=1,
    )
    grads_back = lax.all_to_all(
        stacked.reshape(rank_count, run_rows, 3 * width_local),
        "seq",
        split_axis=0,
        concat_axis=0,
        tiled=True,
    )
    grad_projected = unpack_rows(grads_back).reshape(row_count, 3, width_local)
    return (output, grad_projected, grad_weight)


def solution(mesh):
    placed = (
        P(("dp", "seq"), None, "tp"),
        P(("dp", "seq")),
        P(("dp", "seq")),
        P("tp", None),
        P(("dp", "seq"), "tp"),
    )
    return jax.shard_map(
        on_device,
        mesh=mesh,
        in_specs=placed,
        out_specs=(P(("dp", "seq"), "tp"), P(("dp", "seq"), None, "tp"), P("tp", None)),
        check_vma=False,
    )
```

profile of v0, /device:TPU:0, one launch (start us, length us, event | category | flops | bytes accessed | tf_op | source)
XLA Modules:
  0.0 506.7 jit_solution(14912209828755416140)
XLA Ops:
  10.5 7.3 %all-to-all-start = ((s32[8,1,64]{2,1,0:T(1,128)}), s32[8,1,64]{2,1,0:T(1,128)S(1)}, u32[]{:S(2)}, u32[]{:S(2)}) async-start(s32[8,1,64]{2,1,0:T(1,128)} %broadcast_in_dim.43), calls=%async_computation | async-start | bytes 8192 | tf_op jit(solution)/shard_map/all_to_all | solution.py:51
  17.8 15.8 %all-gather.2.cloned.1.call-done = bf16[256,2048]{1,0:T(8,128)(2,1)} async-done(((bf16[256,1024]{1,0:T(8,128)(2,1)}), bf16[256,2048]{1,0:T(8,128)(2,1)}) %all-gather.2.cloned.1.call-update) | async-done | bytes 1048592 | tf_op jit(solution)/shard_map/all_gather | solution.py:97
  33.6 3.8 convolution_convert_fusion.4
  38.4 1.6 copy.65
  40.0 5.5 %all-to-all-start.3 = ((bf16[8,64,1024]{2,1,0:T(8,128)(2,1)}), bf16[8,64,1024]{2,1,0:T(8,128)(2,1)S(1)}, u32[]{:S(2)}, u32[]{:S(2)}) async-start(bf16[8,64,1024]{2,1,0:T(8,128)(2,1)} %copy.65), calls=%async_computation.4 | async-start | bytes 2097152 | tf_op jit(solution)/shard_map/all_to_all | solution.py:109
  45.5 2.8 copy.62
  48.2 3.2 reshape_reshape.6
  51.4 2.7 convolution_convert_fusion
  54.1 3.4 copy.63
  57.5 13.7 %all-to-all-done.3 = bf16[8,64,1024]{2,1,0:T(8,128)(2,1)S(1)} async-done(((bf16[8,64,1024]{2,1,0:T(8,128)(2,1)}), bf16[8,64,1024]{2,1,0:T(8,128)(2,1)S(1)}, u32[]{:S(2)}, u32[]{:S(2)}) %all-to-all-start.3) | async-done | bytes 1048608 | tf_op jit(solution)/shard_map/all_to_all | solution.py:109
  72.2 14.5 %all-to-all-start.1 = ((bf16[8,64,3072]{2,1,0:T(8,128)(2,1)}), bf16[8,64,3072]{2,1,0:T(8,128)(2,1)S(1)}, u32[]{:S(2)}, u32[]{:S(2)}) async-start(bf16[8,64,3072]{2,1,0:T(8,128)(2,1)} %copy.63), calls=%async_computation.1 | async-start | bytes 6291456 | tf_op jit(solution)/shard_map/all_to_all | solution.py:50
  88.0 2.1 fusion.199
  90.2 1.7 copy.116
  91.8 1.7 copy.117
  93.5 1.7 copy.118
  95.2 1.7 copy.119
  96.8 1.7 copy.120
  100.2 57.3 %all-to-all-done.1 = bf16[8,64,3072]{2,1,0:T(8,128)(2,1)S(1)} async-done(((bf16[8,64,3072]{2,1,0:T(8,128)(2,1)}), bf16[8,64,3072]{2,1,0:T(8,128)(2,1)S(1)}, u32[]{:S(2)}, u32[]{:S(2)}) %all-to-all-start.1) | async-done | bytes 3145760 | tf_op jit(solution)/shard_map/all_to_all | solution.py:50
  157.5 6.0 %reshape.86 = bf16[512,3,1024]{2,1,0:T(4,128)(2,1)} reshape(bf16[8,64,3072]{2,1,0:T(8,128)(2,1)S(1)} %all-to-all-done.1) | data formatting | bytes 6291456 | tf_op jit(solution)/shard_map/reshape | solution.py:53
  163.5 3.1 fusion.198
  166.6 8.5 %fusion.197 = (bf16[512,1,128]{2,1,0:T(2,128)(2,1)S(1)}, bf16[512,1,128]{2,1,0:T(2,128)(2,1)S(1)}, bf16[512,1,128]{2,1,0:T(2,128)(2,1)S(1)}, bf16[512,1,128]{2,1...) fusion(bf16[512,3,1024]{2,1,0:T(4,128)(2,1)} %reshape.86), kind=kLoop, calls=%fused_computation.289 | loop fusion | bytes 4980736 | tf_op jit(solution)/shard_map/slice | solution.py:62
  189.9 1.1 fusion.9
  194.6 1.1 constant_dynamic-update-slice_fusion
  195.7 2.3 copy.64
  197.9 3.6 all-to-all-start.2
  202.7 2.1 fusion.29
  204.8 1.5 fusion.45
  206.3 1.7 fusion.8
  212.2 15.2 %all-to-all-done.2 = bf16[8,64,1024]{2,1,0:T(8,128)(2,1)S(1)} async-done(((bf16[8,64,1024]{2,1,0:T(8,128)(2,1)}), bf16[8,64,1024]{2,1,0:T(8,128)(2,1)S(1)}, u32[]{:S(2)}, u32[]{:S(2)}) %all-to-all-start.2) | async-done | bytes 1048608 | tf_op jit(solution)/shard_map/all_to_all | solution.py:85
  228.9 6.1 %fusion.225 = f32[1024,2048]{1,0:T(8,128)} fusion(bf16[256,1024]{1,0:T(8,128)(2,1)S(1)} %reshape.89, bf16[256,2048]{1,0:T(8,128)(2,1)} %all-gather.2.cloned.1.call-done), kind=kOutput, calls=%fused_computation.301 | convolution fusion | flops 1073741824 | bytes 9961472 | tf_op jit(solution)/shard_map/dot_general | solution.py:101
  235.1 1.5 fusion.47
  236.6 1.1 fusion.52
  237.8 1.0 fusion.51
  241.8 1.0 fusion.48
  243.4 1.6 pad_maximum_fusion
  245.0 5.7 %copy.82 = bf16[512,3,1024]{2,1,0:T(4,128)(2,1)} copy(bf16[512,3,1024]{0,2,1:T(8,128)(2,1)S(1)} %pad_maximum_fusion) | data formatting | bytes 6291456 | tf_op jit(solution)/shard_map/stack | solution.py:151
  250.7 9.7 %reshape.93 = bf16[8,64,3072]{2,1,0:T(8,128)(2,1)} reshape(bf16[512,3,1024]{2,1,0:T(4,128)(2,1)} %copy.82) | data formatting | bytes 6291456 | tf_op jit(solution)/shard_map/reshape | solution.py:160
  260.4 3.7 all-to-all-start.4
  264.3 5.0 fusion.224
  269.4 92.6 %all-to-all-done.4 = bf16[8,64,3072]{2,1,0:T(8,128)(2,1)S(1)} async-done(((bf16[8,64,3072]{2,1,0:T(8,128)(2,1)}), bf16[8,64,3072]{2,1,0:T(8,128)(2,1)S(1)}, u32[]{:S(2)}, u32[]{:S(2)}) %all-to-all-start.4) | async-done | bytes 3145760 | tf_op jit(solution)/shard_map/all_to_all | solution.py:159
  362.0 1.7 copy.125
  363.7 1.0 convolution_convert_fusion.1
  364.7 2.6 reshape_reshape.7
  367.3 3.3 copy.83
  370.6 93.0 %all-reduce.2.cloned.1.call-done = f32[1024,2048]{1,0:T(8,128)} async-done(((f32[1024,2048]{1,0:T(8,128)}), f32[1024,2048]{1,0:T(8,128)}) %all-reduce.2.cloned.1.call-update) | async-done | bytes 8388624 | tf_op jit(solution)/shard_map/psum | solution.py:107
  463.6 8.4 %broadcast_multiply_fusion = f32[1024,2048]{1,0:T(8,128)} fusion(f32[1024,2048]{1,0:T(8,128)} %all-reduce.2.cloned.1.call-done), kind=kLoop, calls=%fused_computation.4 | loop fusion | flops 2097152 | bytes 16777216 | tf_op jit(solution)/shard_map/mul | solution.py:107
  472.0 25.6 %reduce-scatter.2.cloned.1.call-done = f32[256,1024]{1,0:T(8,128)} async-done(((f32[256,2048]{1,0:T(8,128)}), f32[256,1024]{1,0:T(8,128)}) %reduce-scatter.2.cloned.1.call-update) | async-done | bytes 1048592 | tf_op jit(solution)/shard_map/reduce_scatter | solution.py:94
  497.6 2.1 convert_element_type.237
  (209 shorter events, 36.7 us)
Async XLA Ops:
  7.2 26.4 %all-gather.2.cloned.1.call-start = ((), (), s32[]{:S(2)}) async-start(), calls=%async_computation.7 | async-start | bytes 1572864 | tf_op jit(solution)/shard_map/all_gather | solution.py:97
  10.5 29.5 %all-to-all-start = ((s32[8,1,64]{2,1,0:T(1,128)}), s32[8,1,64]{2,1,0:T(1,128)S(1)}, u32[]{:S(2)}, u32[]{:S(2)}) async-start(s32[8,1,64]{2,1,0:T(1,128)} %broadcast_in_dim.43), calls=%async_computation | async-start | bytes 8192 | tf_op jit(solution)/shard_map/all_to_all | solution.py:51
  40.0 31.3 %all-to-all-start.3 = ((bf16[8,64,1024]{2,1,0:T(8,128)(2,1)}), bf16[8,64,1024]{2,1,0:T(8,128)(2,1)S(1)}, u32[]{:S(2)}, u32[]{:S(2)}) async-start(bf16[8,64,1024]{2,1,0:T(8,128)(2,1)} %copy.65), calls=%async_computation.4 | async-start | bytes 2097152 | tf_op jit(solution)/shard_map/all_to_all | solution.py:109
  72.2 85.3 %all-to-all-start.1 = ((bf16[8,64,3072]{2,1,0:T(8,128)(2,1)}), bf16[8,64,3072]{2,1,0:T(8,128)(2,1)S(1)}, u32[]{:S(2)}, u32[]{:S(2)}) async-start(bf16[8,64,3072]{2,1,0:T(8,128)(2,1)} %copy.63), calls=%async_computation.1 | async-start | bytes 6291456 | tf_op jit(solution)/shard_map/all_to_all | solution.py:50
  88.0 92.1 %copy-start.62 = (s32[512]{0:T(512)}, s32[512]{0:T(512)S(1)}, u32[]{:S(2)}) copy-start(s32[512]{0:T(512)S(1)} %eq.34) | copy-start | bytes 6148
  175.1 13.2 %copy-start.23 = (bf16[512,1,128]{2,1,0:T(2,128)(2,1)}, bf16[512,1,128]{2,1,0:T(2,128)(2,1)S(1)}, u32[]{:S(2)}) copy-start(bf16[512,1,128]{2,1,0:T(2,128)(2,1)S(1)} %get-tuple-element.20) | copy-start | bytes 393220
  175.1 13.2 %copy-start.35 = (bf16[512,1,128]{2,1,0:T(2,128)(2,1)}, bf16[512,1,128]{2,1,0:T(2,128)(2,1)S(1)}, u32[]{:S(2)}) copy-start(bf16[512,1,128]{2,1,0:T(2,128)(2,1)S(1)} %get-tuple-element.19) | copy-start | bytes 393220
  175.1 18.9 %copy-start.32 = (bf16[512,1,128]{2,1,0:T(2,128)(2,1)}, bf16[512,1,128]{2,1,0:T(2,128)(2,1)S(1)}, u32[]{:S(2)}) copy-start(bf16[512,1,128]{2,1,0:T(2,128)(2,1)S(1)} %get-tuple-element.16) | copy-start | bytes 393220
  175.2 19.4 %copy-start.34 = (bf16[512,1,128]{2,1,0:T(2,128)(2,1)}, bf16[512,1,128]{2,1,0:T(2,128)(2,1)S(1)}, u32[]{:S(2)}) copy-start(bf16[512,1,128]{2,1,0:T(2,128)(2,1)S(1)} %get-tuple-element.15) | copy-start | bytes 393220
  175.5 2.1 copy-start.5
  175.5 1.7 copy-start.1
  178.5 1.6 copy-start.9
  178.5 1.6 copy-start.38
  178.7 1.4 copy-start.40
  180.5 1.6 copy-start.13
  180.5 1.6 copy-start.46
  180.7 1.4 copy-start.48
  182.7 1.6 copy-start.7
  184.7 1.6 copy-start.11
  184.7 1.6 copy-start.42
  186.6 1.6 copy-start.15
  186.6 1.6 copy-start.50
  188.6 2.4 copy-start.17
  188.7 2.4 copy-start.54
  188.9 2.2 copy-start.56
  193.7 2.0 copy-start.21
  194.4 3.6 copy-start.19
  197.9 29.5 %all-to-all-start.2 = ((bf16[8,64,1024]{2,1,0:T(8,128)(2,1)}), bf16[8,64,1024]{2,1,0:T(8,128)(2,1)S(1)}, u32[]{:S(2)}, u32[]{:S(2)}) async-start(bf16[8,64,1024]{2,1,0:T(8,128)(2,1)} %bitcast.1), calls=%async_computation.2 | async-start | bytes 2097152 | tf_op jit(solution)/shard_map/all_to_all | solution.py:85
  201.5 262.1 %all-reduce.2.cloned.1.call-start = ((), (), s32[]{:S(2)}) async-start(), calls=%async_computation.8 | async-start | bytes 16777216 | tf_op jit(solution)/shard_map/psum | solution.py:107
  202.7 5.2 %copy-start.33 = (bf16[512,1,128]{2,1,0:T(2,128)(2,1)S(1)}, bf16[512,1,128]{2,1,0:T(2,128)(2,1)}, u32[]{:S(2)}) copy-start(bf16[512,1,128]{2,1,0:T(2,128)(2,1)} %copy-done.32) | copy-start | bytes 393220
  204.8 4.1 copy-start.6
  207.9 3.0 copy-start.24
  208.0 2.0 copy-start.10
  208.0 2.0 copy-start.39
  208.0 1.9 copy-start.41
  228.9 6.1 %copy-start.2 = (bf16[256,1024]{1,0:T(8,128)(2,1)}, bf16[256,1024]{1,0:T(8,128)(2,1)S(1)}, u32[]{:S(2)}) copy-start(bf16[256,1024]{1,0:T(8,128)(2,1)S(1)} %reshape.89) | copy-start | bytes 1572868
  235.0 1.6 copy-start.8
  235.0 1.6 copy-start.37
  235.1 2.7 copy-start.12
  235.1 2.7 copy-start.43
  235.1 2.7 copy-start.45
  236.6 2.2 copy-start.3
  237.7 1.5 copy-start.16
  237.8 1.5 copy-start.51
  237.8 1.5 copy-start.53
  241.8 1.6 copy-start.22
  260.4 101.6 %all-to-all-start.4 = ((bf16[8,64,3072]{2,1,0:T(8,128)(2,1)}), bf16[8,64,3072]{2,1,0:T(8,128)(2,1)S(1)}, u32[]{:S(2)}, u32[]{:S(2)}) async-start(bf16[8,64,3072]{2,1,0:T(8,128)(2,1)} %reshape.93), calls=%async_computation.5 | async-start | bytes 6291456 | tf_op jit(solution)/shard_map/all_to_all | solution.py:159
  264.0 233.6 %reduce-scatter.2.cloned.1.call-start = ((), (), s32[]{:S(2)}) async-start(), calls=%async_computation.6 | async-start | bytes 3145728 | tf_op jit(solution)/shard_map/reduce_scatter | solution.py:94
  (24 other events, 29.2 us)
Sparse Core Ops, SparseCore 0:
  9.5 23.9 all-gather.1
  235.2 228.3 all-reduce.1
  465.9 31.6 reduce-scatter.1
where the time goes:
time: 510 us; the launch traced here: 507 us
  waiting for transfers between devices  314 us (62%)
  local copies, waits for them, and re-layouts  74 us (15%)
  matrix products  52.7 us (10%)
  starting transfers between devices  35.1 us (7%)
  other arithmetic  15.9 us (3%)
  between operations  15.1 us (3%)
    psum x1, waiting for transfers between devices, on_device(): lax.psum(grad_block, ('dp', 'seq')) * (1.0 / math.sqrt(row_total))  93 us
    all_to_all x1, waiting for transfers between devices, on_device(): lax.all_to_all(stacked.reshape(rank_count, run_rows, 3 * width_local), 's...  92.6 us
    all_to_all x1, waiting for transfers between devices, on_device(): lax.all_to_all(packed_send, 'seq', split_axis=0, concat_axis=0, tiled=True)  57.3 us
    reduce_scatter x1, waiting for transfers between devices, on_device(): lax.psum_scatter(partial_terms, 'tp', scatter_dimension=1, tiled=True)  25.6 us
    unnamed x141, local copies, waits for them, and re-layouts  24.1 us
    all_gather x1, waiting for transfers between devices, on_device(): shard_cols = lax.all_gather(grad_output, 'tp', axis=1, tiled=True)  15.8 us
    all_to_all x1, waiting for transfers between devices, on_device(): lax.all_to_all(attended.reshape(rank_count, run_rows, width_local), 'seq'...  15.2 us
    all_to_all x1, starting transfers between devices, on_device(): lax.all_to_all(packed_send, 'seq', split_axis=0, concat_axis=0, tiled=True)  14.5 us
  transfers between devices with their start and end apart: 8, of which 7 were waited for; matrix products, arithmetic and copies ran while one was open for 18% of the time, Pallas kernels for 0%

commit v1 on v0

--- a/solution.py
+++ b/solution.py
@@ -1,17 +1,244 @@
+import functools
 import math
 
 import jax
 import jax.numpy as jnp
 from jax import lax
+from jax.experimental import pallas as pl
+from jax.experimental.pallas import tpu as pltpu
 from jax.sharding import PartitionSpec as P
 
 HD = 128
+NEG = -1e30
+BF = jnp.bfloat16
+F32 = jnp.float32
+
+
+def _dot(a, b, ca, cb):
+    return lax.dot_general(a, b, (((ca,), (cb,)), ((), ())), preferred_element_type=F32)
+
+
+def _attend_kernel(backward, ranks, run_count, run_rows, counts, order, gathers, *refs):
+    if backward:
+        x_ref, a_ref, g_ref, out_ref, key_acc, value_acc = refs
+    else:
+        x_ref, out_ref = refs
+    scaling = 1.0 / math.sqrt(HD)
+
+    def at(index):
+        run = order[index]
+        source = run // run_count
+        start = pl.multiple_of((run % run_count) * run_rows, run_rows)
+        return source, pl.ds(start, run_rows)
+
+    def variant(rank, runs, query_runs):
+        base = rank * ranks
+        keys = runs * run_rows
+        places = [at(base + j) for j in range(runs)]
+        take = lambda part, span: jnp.concatenate([x_ref[s, part, d, :] for s, d in span], axis=0)
+        key_all = take(1, places)
+        value_all = take(2, places)
+        lane_run = lax.broadcasted_iota(jnp.int32, (1, keys), 1) // run_rows
+        key_gather = jnp.full((1, keys), gathers[base], jnp.int32)
+        for j in range(1, runs):
+            key_gather = jnp.where(lane_run == j, gathers[base + j], key_gather)
+        for first in range(0, runs, query_runs):
+            span = places[first : first + query_runs]
+            query = take(0, span)
+            bias = jnp.concatenate(
+                [
+                    jnp.broadcast_to(
+                        jnp.where(key_gather == gathers[base + first + j], 0.0, NEG).astype(F32),
+                        (run_rows, keys),
+                    )
+                    for j in range(query_runs)
+                ],
+                axis=0,
+            )
+            scores = _dot(query, key_all, 1, 1) * scaling + bias
+            peak = jnp.max(scores, axis=1, keepdims=True)
+            raised = jnp.exp(scores - peak)
+            probs = raised * (1.0 / jnp.sum(raised, axis=1, keepdims=True))
+            low = probs.astype(BF)
+            if not backward:
+                result = _dot(low, value_all, 1, 0).astype(BF)
+                for j, (s, d) in enumerate(span):
+
+                    @pl.when(first + j < counts[rank])
+                    def _(s=s, d=d, j=j):
+                        out_ref[s, d, :] = result[j * run_rows : (j + 1) * run_rows]
+
+                continue
+            grad = jnp.concatenate([g_ref[s, d, :] for s, d in span], axis=0)
+            kept = jnp.concatenate([a_ref[s, d, :] for s, d in span], axis=0)
+            grad_probs = _dot(grad, value_all, 1, 1)
+            delta = jnp.sum(grad.astype(F32) * kept.astype(F32), axis=1, keepdims=True)
+            grad_scores = (probs * (grad_probs - delta)).astype(BF)
+            query_grad = (_dot(grad_scores, key_all, 1, 0) * scaling).astype(BF)
+            for j, (s, d) in enumerate(span):
+
+                @pl.when(first + j < counts[rank])
+                def _(s=s, d=d, j=j):
+                    out_ref[s, 0, d, :] = query_grad[j * run_rows : (j + 1) * run_rows]
+
+            key_part = _dot(grad_scores, query, 0, 0)
+            value_part = _dot(low, grad, 0, 0)
+            if first + query_runs < runs:
+                if first == 0:
+                    key_acc[...] = key_part
+                    value_acc[...] = value_part
+                else:
+                    key_acc[...] += key_part
+                    value_acc[...] += value_part
+                continue
+            if first > 0:
+                key_part = key_part + key_acc[...]
+                value_part = value_part + value_acc[...]
+            key_grad = (key_part * scaling).astype(BF)
+            value_grad = value_part.astype(BF)
+            for j, (s, d) in enumerate(places):
+
+                @pl.when(j < counts[rank])
+                def _(s=s, d=d, j=j):
+                    rows = slice(j * run_rows, (j + 1) * run_rows)
+                    out_ref[s, 1, d, :] = key_grad[rows]
+                    out_ref[s, 2, d, :] = value_grad[rows]
+
+    half = max(ranks // 2, 1)
+
+    @pl.loop(0, ranks)
+    def _(rank):
+        @pl.when((counts[rank] > 0) & (counts[rank] <= half))
+        def _():
+            variant(rank, half, half)
+
+        @pl.when(counts[rank] > half)
+        def _():
+            variant(rank, ranks, half)
+
+
+def attend(backward, ranks, run_count, run_rows, tables, *arrays):
+    rows = run_count * run_rows
+    shape = (ranks, 3, rows, HD) if backward else (ranks, rows, HD)
+    vmem = pl.BlockSpec(memory_space=pltpu.VMEM)
+    scratch = [pltpu.VMEM((ranks * run_rows, HD), F32)] * 2 if backward else []
+    return pl.pallas_call(
+        functools.partial(_attend_kernel, backward, ranks, run_count, run_rows),
+        out_shape=jax.ShapeDtypeStruct(shape, BF),
+        grid_spec=pltpu.PrefetchScalarGridSpec(
+            num_scalar_prefetch=3,
+            grid=(),
+            in_specs=[vmem] * len(arrays),
+            out_specs=vmem,
+            scratch_shapes=scratch,
+        ),
+        compiler_params=pltpu.CompilerParams(vmem_limit_bytes=40 * 1024 * 1024),
+        cost_estimate=pl.CostEstimate(
+            flops=(6 if backward else 2) * 10**8, bytes_accessed=3 * 10**6, transcendentals=10**6
+        ),
+        name="attend_back" if backward else "attend",
+    )(*tables, *arrays)
+
+
+def run_tables(run_target, run_gather, ranks):
+    runs = run_target.shape[0]
+    rank_ids = jnp.arange(ranks, dtype=jnp.int32)
+    named = run_target[None, :] == rank_ids[:, None]
+    counts = jnp.sum(named.astype(jnp.int32), axis=1)
+    run_ids = jnp.arange(runs, dtype=jnp.int32)
+    earlier = named[:, None, :] & (run_ids[None, None, :] < run_ids[None, :, None])
+    place = jnp.sum(earlier.astype(jnp.int32), axis=2)
+    hit = named[:, None, :] & (place[:, None, :] == rank_ids[None, :, None])
+    order = jnp.sum(jnp.where(hit, run_ids, 0), axis=2)
+    gathers = jnp.sum(jnp.where(hit, run_gather + 1, 0), axis=2) - 1
+    return counts, order.reshape(-1), gathers.reshape(-1)
+
+
+def swap_gather(values, axis_name):
+    if lax.axis_size(axis_name) != 2:
+        return lax.all_gather(values, axis_name, axis=1, tiled=True)
+    other = lax.ppermute(values, axis_name, [(0, 1), (1, 0)])
+    first = lax.axis_index(axis_name) == 0
+    return jnp.where(
+        first,
+        jnp.concatenate([values, other], axis=1),
+        jnp.concatenate([other, values], axis=1),
+    )
+
+
+def on_device(projected, destinations, gather_ids, out_weight, grad_output):
+    ranks = lax.axis_size("seq")
+    row_count = projected.shape[0]
+    run_rows = 2 * row_count // ranks
+    run_count = row_count // run_rows
+    width = projected.shape[2]
+    exchange = functools.partial(
+        lax.all_to_all, axis_name="seq", split_axis=0, concat_axis=0, tiled=True
+    )
+    run_info = jnp.stack(
+        [
+            destinations.reshape(run_count, run_rows)[:, 0],
+            gather_ids.reshape(run_count, run_rows)[:, 0],
+        ]
+    )
+    info = exchange(jnp.broadcast_to(run_info[None], (ranks, 2, run_count)))
+    info = info.transpose(1, 0, 2).reshape(2, ranks * run_count)
+    x = projected.transpose(1, 0, 2).reshape(3, row_count, ranks, HD).transpose(2, 0, 1, 3)
+    x = exchange(x)
+    tables = run_tables(info[0], info[1], ranks)
+
+    columns = swap_gather(grad_output, "tp")
+    grad_rows = _dot(columns, out_weight, 1, 1).astype(BF)
+    g = exchange(grad_rows.reshape(row_count, ranks, HD).transpose(1, 0, 2))
+
+    attended = attend(False, ranks, run_count, run_rows, tables, x)
+    attended_rows = exchange(attended).transpose(1, 0, 2).reshape(row_count, width)
+    back = attend(True, ranks, run_count, run_rows, tables, x, attended, g)
+    grads = exchange(back)
+    grad_projected = grads.transpose(1, 2, 0, 3).reshape(3, row_count, width).transpose(1, 0, 2)
+
+    output = project(attended_rows, out_weight)
+    product = _dot(attended_rows, columns, 0, 0)
+    row_total = row_count * lax.axis_size("dp") * ranks
+    grad_weight = total_over_rows(product, 1.0 / math.sqrt(row_total))
+    return output, grad_projected, grad_weight
+
+
+def project(attended_rows, out_weight):
+    partial_terms = _dot(attended_rows, out_weight, 1, 0)
+    if lax.axis_size("tp") != 2:
+        return lax.psum_scatter(partial_terms, "tp", scatter_dimension=1, tiled=True).astype(BF)
+    half = out_weight.shape[1] // 2
+    first = lax.axis_index("tp") == 0
+    mine = jnp.where(first, partial_terms[:, :half], partial_terms[:, half:])
+    sent = jnp.where(first, partial_terms[:, half:], partial_terms[:, :half]).astype(BF)
+    other = lax.ppermute(sent, "tp", [(0, 1), (1, 0)])
+    return (mine + other.astype(F32)).astype(BF)
+
+
+def total_over_rows(product, factor):
+    ranks = lax.axis_size("seq")
+    half, columns = product.shape[0] // 2, product.shape[1]
+    first = lax.axis_index("dp") == 0
+    pairs = [(0, 1), (1, 0)]
+    mine = jnp.where(first, product[:half], product[half:])
+    sent = jnp.where(first, product[half:], product[:half]).astype(BF)
+    mine = mine + lax.ppermute(sent, "dp", pairs).astype(F32)
+    blocks = mine.astype(BF).reshape(ranks, half // ranks, columns)
+    blocks = lax.all_to_all(blocks, "seq", split_axis=0, concat_axis=0, tiled=True)
+    total = (jnp.sum(blocks.astype(F32), axis=0) * factor).astype(BF)
+    total = lax.all_gather(total, "seq", axis=0, tiled=True)
+    other = lax.ppermute(total, "dp", pairs)
+    both = jnp.where(
+        first, jnp.concatenate([total, other]), jnp.concatenate([other, total])
+    )
+    return both.astype(F32)
 
 
 masked_score = -1e30
 
 
-def on_device(projected, destinations, gather_ids, out_weight, grad_output):
+def packed_on_device(projected, destinations, gather_ids, out_weight, grad_output):
     rank_count = lax.axis_size("seq")
     row_count = projected.shape[0]
     run_rows = 2 * row_count // rank_count
@@ -175,8 +402,9 @@
         P("tp", None),
         P(("dp", "seq"), "tp"),
     )
+    whole_heads = 2048 // HD // mesh.shape["tp"] == mesh.shape["seq"]
     return jax.shard_map(
-        on_device,
+        on_device if whole_heads else packed_on_device,
         mesh=mesh,
         in_specs=placed,
         out_specs=(P(("dp", "seq"), "tp"), P(("dp", "seq"), None, "tp"), P("tp", None)),

time: 510 us -> 258 us (0.51)
  waiting for transfers between devices: 314 us -> 91 us
  blocking collectives: 0 us -> 77.4 us
  local copies, waits for them, and re-layouts: 74 us -> 10.1 us
  matrix products: 52.7 us -> 10.6 us
  Pallas kernels: 0 us -> 21 us
  starting transfers between devices: 35.1 us -> 21.3 us
    all_to_all x5 -> x4, waiting for transfers between devices: 179 us -> 62.7 us  [the longest x1 34.9 us: on_device(): x = exchange(x)]
    psum x1 -> x0, waiting for transfers between devices: 93 us -> none  [on_device(): lax.psum(grad_block, ('dp', 'seq')) * (1.0 / math.sqrt(row_total))]
    all_to_all x0 -> x2, blocking collectives: none -> 77.4 us  [the longest x1 52.8 us: total_over_rows(): lax.all_to_all(blocks, 'seq', split_axis=0, concat_axis=0, tiled=True)]
    dot_general x55 -> x3, matrix products: 52.7 us -> 10.6 us  [_dot(): lax.dot_general(a, b, (((ca,), (cb,)), ((), ())), preferred_element_type=...]
    reduce_scatter x1 -> x0, waiting for transfers between devices: 25.6 us -> none  [on_device(): lax.psum_scatter(partial_terms, 'tp', scatter_dimension=1, tiled=True)]
    pallas_call x0 -> x2, Pallas kernels: none -> 21 us  [attend(): pl.pallas_call(functools.partial(_attend_kernel, backward, ranks, run_cou...]
    unnamed x141 -> x4, local copies, waits for them, and re-layouts: 24.1 us -> 3.45 us
    reshape x8 -> x5, local copies, waits for them, and re-layouts: 23 us -> 3.44 us  [the longest x1 1.57 us: on_device(): projected.transpose(1, 0, 2).reshape(3, row_count, ranks, HD)]
  transfers between devices with their start and end apart: 8 -> 9, of which waited for: 7 -> 7; matrix products, arithmetic and copies ran while one was open for 18% -> 7% of each run, Pallas kernels for 0% -> 5%
where the time goes in v1:
time: 258 us; the launch traced here: 257 us
  waiting for transfers between devices  91 us (35%)
  blocking collectives  77.4 us (30%)
  starting transfers between devices  21.3 us (8%)
  Pallas kernels  21 us (8%)
  between operations  14.2 us (6%)
  other arithmetic  11.2 us (4%)
  matrix products  10.6 us (4%)
  local copies, waits for them, and re-layouts  10.1 us (4%)
    all_to_all x1, blocking collectives, total_over_rows(): lax.all_to_all(blocks, 'seq', split_axis=0, concat_axis=0, tiled=True)  52.8 us
    all_to_all x1, waiting for transfers between devices, on_device(): x = exchange(x)  34.9 us
    all_to_all x1, blocking collectives, on_device(): g = exchange(grad_rows.reshape(row_count, ranks, HD).transpose(1, 0, 2))  24.6 us
    pallas_call x2, Pallas kernels, attend(): pl.pallas_call(functools.partial(_attend_kernel, backward, ranks, run_cou...  21 us
    all_to_all x1, waiting for transfers between devices, on_device(): exchange(attended).transpose(1, 0, 2).reshape(row_count, width)  12.9 us
    ppermute x1, waiting for transfers between devices, project(): other = lax.ppermute(sent, 'tp', [(0, 1), (1, 0)])  12.9 us
    all_to_all x1, waiting for transfers between devices, on_device(): grads = exchange(back)  11.7 us
    all_gather x1, waiting for transfers between devices, total_over_rows(): total = lax.all_gather(total, 'seq', axis=0, tiled=True)  11.2 us
  transfers between devices with their start and end apart: 9, of which 7 were waited for; matrix products, arithmetic and copies ran while one was open for 7% of the time, Pallas kernels for 5%

profile of v1, /device:TPU:0, one launch (start us, length us, event | category | flops | bytes accessed | tf_op | source)
XLA Modules:
  0.0 256.8 jit_solution(12956243438789504553)
XLA Ops:
  7.2 0.8 reshape.77
  7.9 0.1 slice_reduce_fusion.2
  8.0 0.8 reshape.78
  8.8 0.1 slice_reduce_fusion.1
  8.9 0.6 broadcast_in_dim.12
  9.5 7.3 %all-to-all-start = ((s32[8,2,4]{2,1,0:T(2,128)}), s32[8,2,4]{2,1,0:T(2,128)S(1)}, u32[]{:S(2)}, u32[]{:S(2)}) async-start(s32[8,2,4]{2,1,0:T(2,128)} %broadcast_in_dim.12), calls=%async_computation | async-start | bytes 16384 | tf_op jit(solution)/shard_map/all_to_all | solution.py:184
  16.8 1.7 copy.29
  18.5 1.6 copy.30
  20.1 3.2 %all-to-all-done = s32[8,2,4]{2,1,0:T(2,128)S(1)} async-done(((s32[8,2,4]{2,1,0:T(2,128)}), s32[8,2,4]{2,1,0:T(2,128)S(1)}, u32[]{:S(2)}, u32[]{:S(2)}) %all-to-all-start) | async-done | bytes 288 | tf_op jit(solution)/shard_map/all_to_all | solution.py:184
  23.3 3.6 %all-to-all-start.1 = ((bf16[8,3,256,128]{3,2,1,0:T(8,128)(2,1)}), bf16[8,3,256,128]{3,2,1,0:T(8,128)(2,1)S(1)}, u32[]{:S(2)}, u32[]{:S(2)}) async-start(bf16[8,3,256,128]{3,2,1,0:T(8,128)(2,1)} %bitcast.3), calls=%async_computation.1 | async-start | bytes 3145728 | tf_op jit(solution)/shard_map/all_to_all | solution.py:187
  27.0 0.1 add.20
  27.0 0.1 eq.40
  27.1 0.2 convert_reduce_fusion.1
  27.4 0.3 select_reduce_fusion
  27.7 0.1 sub.7.gathers
  27.8 0.1 reshape.79.order
  27.9 0.1 convert_reduce_fusion.2.counts
  28.0 34.9 %all-to-all-done.1.refs_0_ = bf16[8,3,256,128]{3,2,1,0:T(8,128)(2,1)S(1)} async-done(((bf16[8,3,256,128]{3,2,1,0:T(8,128)(2,1)}), bf16[8,3,256,128]{3,2,1,0:T(8,128)(2,1)S(1)}, u32[]{:S(2)}, u32[]{:S(2)}) %all-to-all-start.1) | async-done | bytes 1572896 | tf_op jit(solution)/shard_map/all_to_all | solution.py:187
  62.9 8.0 %attend.1.refs_1_ = bf16[8,256,128]{2,1,0:T(8,128)(2,1)} custom-call(s32[8]{0:T(128)S(1)} %convert_reduce_fusion.2.counts, s32[64]{0:T(128)S(1)} %reshape.79.order, s32[64]{0:T(128)S(1)} %sub.7.gathers, bf16[8,3,256,128]{3,2,1,0:T(8,128)(2,1)S(1)} %all-to-all-done.1.refs_0_), custom_call_target="tpu_custom_call" | custom-call | flops 200000000 | bytes 3000000 | tf_op jit(solution)/shard_map/attend/pallas_call | solution.py:125
  70.9 3.5 %all-to-all-start.2 = ((bf16[8,256,128]{2,1,0:T(8,128)(2,1)}), bf16[8,256,128]{2,1,0:T(8,128)(2,1)S(1)}, u32[]{:S(2)}, u32[]{:S(2)}) async-start(bf16[8,256,128]{2,1,0:T(8,128)(2,1)} %attend.1.refs_1_), calls=%async_computation.2 | async-start | bytes 1048576 | tf_op jit(solution)/shard_map/all_to_all | solution.py:195
  74.4 0.0 all-gather.2.cloned.1.call-start
  74.4 1.6 collective-permute-start.1
  76.0 12.9 %all-to-all-done.2 = bf16[8,256,128]{2,1,0:T(8,128)(2,1)S(1)} async-done(((bf16[8,256,128]{2,1,0:T(8,128)(2,1)}), bf16[8,256,128]{2,1,0:T(8,128)(2,1)S(1)}, u32[]{:S(2)}, u32[]{:S(2)}) %all-to-all-start.2) | async-done | bytes 524320 | tf_op jit(solution)/shard_map/all_to_all | solution.py:195
  88.9 0.2 copy.31
  89.2 2.5 fusion.1
  91.7 0.4 select_convert_fusion
  92.1 0.1 collective-permute-start.2
  92.1 4.1 %collective-permute-done.2 = bf16[512,2048]{1,0:T(8,128)(2,1)S(1)} collective-permute-done((bf16[512,2048]{1,0:T(8,128)(2,1)S(1)}, bf16[512,2048]{1,0:T(8,128)(2,1)S(1)}, u32[]{:S(2)}, u32[]{:S(2)}) %collective-permute-start.2) | collective-permute-done | bytes 2097184 | tf_op jit(solution)/shard_map/ppermute | solution.py:226
  96.3 1.2 add_convert_fusion
  97.5 52.8 %all_to_all.30 = bf16[8,64,2048]{2,1,0:T(8,128)(2,1)S(1)} all-to-all(bf16[8,64,2048]{2,1,0:T(8,128)(2,1)S(1)} %bitcast.20), channel_id=1, replica_groups=mesh['dp'=2,'seq'=8,'tp'=2] {'seq'}, dimensions={0} | all-to-all | bytes 4194304 | tf_op jit(solution)/shard_map/all_to_all | solution.py:228
  150.3 0.3 convert_reduce_fusion
  150.7 0.7 multiply_convert_fusion
  151.5 4.6 %convolution_convert_fusion = bf16[256,1024]{1,0:T(8,128)(2,1)} fusion(bf16[1024,2048]{1,0:T(8,128)(2,1)} %param.8, bf16[256,1024]{1,0:T(8,128)(2,1)} %collective-permute-done.1, bf16[256,1024]{1,0:T(8,128)(2,1)S(1)} %copy-done, pred[]{:T(512)S(6)} %eq.39), kind=kOutput, calls=%fused_computation.5 | convolution fusion | flops 1078722560 | bytes 5767169 | tf_op jit(solution)/shard_map/dot_general | solution.py:18
  156.1 1.2 copy.32
  157.3 0.3 copy.33
  157.6 24.6 %all_to_all.31.refs_2_ = bf16[8,256,128]{2,1,0:T(8,128)(2,1)S(1)} all-to-all(bf16[8,256,128]{2,1,0:T(8,128)(2,1)S(1)} %bitcast.28), channel_id=1, replica_groups=mesh['dp'=2,'seq'=8,'tp'=2] {'seq'}, dimensions={0} | all-to-all | bytes 1048576 | tf_op jit(solution)/shard_map/all_to_all | solution.py:192
  182.2 12.9 %attend_back.1 = bf16[8,3,256,128]{3,2,1,0:T(8,128)(2,1)} custom-call(s32[8]{0:T(128)S(1)} %convert_reduce_fusion.2.counts, s32[64]{0:T(128)S(1)} %reshape.79.order, s32[64]{0:T(128)S(1)} %sub.7.gathers, bf16[8,3,256,128]{3,2,1,0:T(8,128)(2,1)S(1)} %all-to-all-done.1.refs_0_, bf16[8,256,128]{2,1,0:T(8,128)(2,1)} %attend.1.refs_1_, ...), custom_call_target="tpu_custom_call" | custom-call | flops 600000000 | bytes 3000000 | tf_op jit(solution)/shard_map/attend_back/pallas_call | solution.py:125
  195.1 3.8 %all-to-all-start.4 = ((bf16[8,3,256,128]{3,2,1,0:T(8,128)(2,1)}), bf16[8,3,256,128]{3,2,1,0:T(8,128)(2,1)S(1)}, u32[]{:S(2)}, u32[]{:S(2)}) async-start(bf16[8,3,256,128]{3,2,1,0:T(8,128)(2,1)} %attend_back.1), calls=%async_computation.4 | async-start | bytes 3145728 | tf_op jit(solution)/shard_map/all_to_all | solution.py:197
  198.9 11.2 %all-gather.2.cloned.1.call-done = bf16[512,2048]{1,0:T(8,128)(2,1)} async-done(((bf16[64,2048]{1,0:T(8,128)(2,1)}), bf16[512,2048]{1,0:T(8,128)(2,1)}) %all-gather.2.cloned.1.call-update) | async-done | bytes 2097168 | tf_op jit(solution)/shard_map/all_gather | solution.py:230
  210.1 3.5 %fusion.6 = f32[256,2048]{1,0:T(8,128)S(1)} fusion(bf16[256,1024]{0,1:T(8,128)(2,1)S(1)} %bitcast.25, bf16[1024,2048]{1,0:T(8,128)(2,1)} %param.8), kind=kOutput, calls=%fused_computation.28 | convolution fusion | flops 1073741824 | bytes 6815744 | tf_op jit(solution)/shard_map/dot_general | solution.py:18
  213.6 0.1 select_convert_fusion.1
  213.7 1.5 collective-permute-start
  215.2 12.9 %collective-permute-done = bf16[256,1024]{1,0:T(8,128)(2,1)S(1)} collective-permute-done((bf16[256,1024]{1,0:T(8,128)(2,1)S(1)}, bf16[256,1024]{1,0:T(8,128)(2,1)S(1)}, u32[]{:S(2)}, u32[]{:S(2)}) %collective-permute-start) | collective-permute-done | bytes 524320 | tf_op jit(solution)/shard_map/ppermute | solution.py:215
  228.1 1.1 add_convert_fusion.1
  229.1 11.7 %all-to-all-done.4 = bf16[8,3,256,128]{3,2,1,0:T(8,128)(2,1)S(1)} async-done(((bf16[8,3,256,128]{3,2,1,0:T(8,128)(2,1)}), bf16[8,3,256,128]{3,2,1,0:T(8,128)(2,1)S(1)}, u32[]{:S(2)}, u32[]{:S(2)}) %all-to-all-start.4) | async-done | bytes 1572896 | tf_op jit(solution)/shard_map/all_to_all | solution.py:197
  240.9 0.7 copy.34
  241.6 1.7 copy.35
  243.3 6.7 %fusion = f32[1024,2048]{1,0:T(8,128)} fusion(bf16[512,2048]{1,0:T(8,128)(2,1)} %collective-permute-done.3, bf16[512,2048]{1,0:T(8,128)(2,1)} %all-gather.2.cloned.1.call-done, pred[]{:T(512)S(6)} %eq.47), kind=kLoop, calls=%fused_computation.1 | loop fusion | flops 20971520 | bytes 12582913 | tf_op jit(solution)/shard_map/convert_element_type | solution.py:235
  (11 shorter events, 0.1 us)
Async XLA Ops:
  9.5 13.8 %all-to-all-start = ((s32[8,2,4]{2,1,0:T(2,128)}), s32[8,2,4]{2,1,0:T(2,128)S(1)}, u32[]{:S(2)}, u32[]{:S(2)}) async-start(s32[8,2,4]{2,1,0:T(2,128)} %broadcast_in_dim.12), calls=%async_computation | async-start | bytes 16384 | tf_op jit(solution)/shard_map/all_to_all | solution.py:184
  23.3 39.6 %all-to-all-start.1 = ((bf16[8,3,256,128]{3,2,1,0:T(8,128)(2,1)}), bf16[8,3,256,128]{3,2,1,0:T(8,128)(2,1)S(1)}, u32[]{:S(2)}, u32[]{:S(2)}) async-start(bf16[8,3,256,128]{3,2,1,0:T(8,128)(2,1)} %bitcast.3), calls=%async_computation.1 | async-start | bytes 3145728 | tf_op jit(solution)/shard_map/all_to_all | solution.py:187
  26.9 47.5 %copy-start = (bf16[256,1024]{1,0:T(8,128)(2,1)S(1)}, bf16[256,1024]{1,0:T(8,128)(2,1)}, u32[]{:S(2)}) copy-start(bf16[256,1024]{1,0:T(8,128)(2,1)} %param.9) | copy-start | bytes 1572868
  70.9 18.0 %all-to-all-start.2 = ((bf16[8,256,128]{2,1,0:T(8,128)(2,1)}), bf16[8,256,128]{2,1,0:T(8,128)(2,1)S(1)}, u32[]{:S(2)}, u32[]{:S(2)}) async-start(bf16[8,256,128]{2,1,0:T(8,128)(2,1)} %attend.1.refs_1_), calls=%async_computation.2 | async-start | bytes 1048576 | tf_op jit(solution)/shard_map/all_to_all | solution.py:195
  74.4 135.7 %all-gather.2.cloned.1.call-start = ((), (), s32[]{:S(2)}) async-start(), calls=%async_computation.6 | async-start | bytes 2359296 | tf_op jit(solution)/shard_map/all_gather | solution.py:230
  74.4 14.7 %collective-permute-start.1 = (bf16[256,1024]{1,0:T(8,128)(2,1)S(1)}, bf16[256,1024]{1,0:T(8,128)(2,1)}, u32[]{:S(2)}, u32[]{:S(2)}) collective-permute-start(bf16[256,1024]{1,0:T(8,128)(2,1)S(1)} %copy-done), channel_id=1, source_target_pairs={{0,1},{1,0},{2,3},{3,2},{4,5},{5,4},{6,7},{7,6},{8,9},{9,8},{10,11... | collective-permute-start | bytes 1572872 | tf_op jit(solution)/shard_map/ppermute | solution.py:160
  92.1 4.2 %collective-permute-start.2 = (bf16[512,2048]{1,0:T(8,128)(2,1)S(1)}, bf16[512,2048]{1,0:T(8,128)(2,1)S(1)}, u32[]{:S(2)}, u32[]{:S(2)}) collective-permute-start(bf16[512,2048]{1,0:T(8,128)(2,1)S(1)} %select_convert_fusion), channel_id=1, source_target_pairs={{0,16},{16,0},{1,17},{17,1},{2,18},{18,2},{3,19},{19,3},{4,20},{20... | collective-permute-start | bytes 6291464 | tf_op jit(solution)/shard_map/ppermute | solution.py:226
  195.1 45.8 %all-to-all-start.4 = ((bf16[8,3,256,128]{3,2,1,0:T(8,128)(2,1)}), bf16[8,3,256,128]{3,2,1,0:T(8,128)(2,1)S(1)}, u32[]{:S(2)}, u32[]{:S(2)}) async-start(bf16[8,3,256,128]{3,2,1,0:T(8,128)(2,1)} %attend_back.1), calls=%async_computation.4 | async-start | bytes 3145728 | tf_op jit(solution)/shard_map/all_to_all | solution.py:197
  210.1 33.2 %collective-permute-start.3 = (bf16[512,2048]{1,0:T(8,128)(2,1)}, bf16[512,2048]{1,0:T(8,128)(2,1)}, u32[]{:S(2)}, u32[]{:S(2)}) collective-permute-start(bf16[512,2048]{1,0:T(8,128)(2,1)} %all-gather.2.cloned.1.call-done), channel_id=1, source_target_pairs={{0,16},{16,0},{1,17},{17,1},{2,18},{18,2},{3,19},{19,3},{4,20},{20... | collective-permute-start | bytes 6291464 | tf_op jit(solution)/shard_map/ppermute | solution.py:231
  213.7 14.4 %collective-permute-start = (bf16[256,1024]{1,0:T(8,128)(2,1)S(1)}, bf16[256,1024]{1,0:T(8,128)(2,1)S(1)}, u32[]{:S(2)}, u32[]{:S(2)}) collective-permute-start(bf16[256,1024]{1,0:T(8,128)(2,1)S(1)} %select_convert_fusion.1), channel_id=1, source_target_pairs={{0,1},{1,0},{2,3},{3,2},{4,5},{5,4},{6,7},{7,6},{8,9},{9,8},{10,11... | collective-permute-start | bytes 1572872 | tf_op jit(solution)/shard_map/ppermute | solution.py:215
Sparse Core Ops, SparseCore 0:
  151.6 58.4 all-gather.1

commit v2 on v1

--- a/solution.py
+++ b/solution.py
@@ -24,6 +24,7 @@
     else:
         x_ref, out_ref = refs
     scaling = 1.0 / math.sqrt(HD)
+    rows = run_count * run_rows
 
     def at(index):
         run = order[index]
@@ -35,7 +36,9 @@
         base = rank * ranks
         keys = runs * run_rows
         places = [at(base + j) for j in range(runs)]
-        take = lambda part, span: jnp.concatenate([x_ref[s, part, d, :] for s, d in span], axis=0)
+        take = lambda part, span: jnp.concatenate(
+            [x_ref[s, pl.ds(part * rows + d.start, run_rows), :] for s, d in span], axis=0
+        )
         key_all = take(1, places)
         value_all = take(2, places)
         lane_run = lax.broadcasted_iota(jnp.int32, (1, keys), 1) // run_rows
@@ -175,64 +178,227 @@
     exchange = functools.partial(
         lax.all_to_all, axis_name="seq", split_axis=0, concat_axis=0, tiled=True
     )
-    run_info = jnp.stack(
+    run_info = jnp.concatenate(
         [
             destinations.reshape(run_count, run_rows)[:, 0],
             gather_ids.reshape(run_count, run_rows)[:, 0],
         ]
     )
-    info = exchange(jnp.broadcast_to(run_info[None], (ranks, 2, run_count)))
-    info = info.transpose(1, 0, 2).reshape(2, ranks * run_count)
-    x = projected.transpose(1, 0, 2).reshape(3, row_count, ranks, HD).transpose(2, 0, 1, 3)
-    x = exchange(x)
-    tables = run_tables(info[0], info[1], ranks)
+    tail = jnp.broadcast_to(jnp.pad(run_info, (0, HD - 2 * run_count))[None, :], (16, HD))
+    x = exchange(split_heads(projected.transpose(1, 0, 2), tail.astype(BF), ranks))
+    info = x[:, 3 * row_count, : 2 * run_count].astype(jnp.int32)
+    run_target = info[:, :run_count].reshape(-1)
+    run_gather = info[:, run_count:].reshape(-1)
+    tables = run_tables(run_target, run_gather, ranks)
 
     columns = swap_gather(grad_output, "tp")
     grad_rows = _dot(columns, out_weight, 1, 1).astype(BF)
-    g = exchange(grad_rows.reshape(row_count, ranks, HD).transpose(1, 0, 2))
+    blocks = head_blocks(grad_rows, ranks)
+    x, blocks, columns = lax.optimization_barrier((x, blocks, columns))
+    g = exchange(blocks)
 
     attended = attend(False, ranks, run_count, run_rows, tables, x)
-    attended_rows = exchange(attended).transpose(1, 0, 2).reshape(row_count, width)
+    attended_rows = exchange(attended)
     back = attend(True, ranks, run_count, run_rows, tables, x, attended, g)
+    attended_rows, back = lax.optimization_barrier((attended_rows, back))
     grads = exchange(back)
-    grad_projected = grads.transpose(1, 2, 0, 3).reshape(3, row_count, width).transpose(1, 0, 2)
-
-    output = project(attended_rows, out_weight)
+    attended_rows = jnp.concatenate([attended_rows[h] for h in range(ranks)], axis=1)
+
+    partial_terms = _dot(attended_rows, out_weight, 1, 0)
     product = _dot(attended_rows, columns, 0, 0)
     row_total = row_count * lax.axis_size("dp") * ranks
-    grad_weight = total_over_rows(product, 1.0 / math.sqrt(row_total))
-    return output, grad_projected, grad_weight
-
-
-def project(attended_rows, out_weight):
-    partial_terms = _dot(attended_rows, out_weight, 1, 0)
-    if lax.axis_size("tp") != 2:
-        return lax.psum_scatter(partial_terms, "tp", scatter_dimension=1, tiled=True).astype(BF)
     half = out_weight.shape[1] // 2
     first = lax.axis_index("tp") == 0
     mine = jnp.where(first, partial_terms[:, :half], partial_terms[:, half:])
     sent = jnp.where(first, partial_terms[:, half:], partial_terms[:, :half]).astype(BF)
-    other = lax.ppermute(sent, "tp", [(0, 1), (1, 0)])
-    return (mine + other.astype(F32)).astype(BF)
-
-
-def total_over_rows(product, factor):
-    ranks = lax.axis_size("seq")
+    other, total = reduce_sums(sent, product, ranks, 1.0 / math.sqrt(row_total))
+    output = (mine + other.astype(F32)).astype(BF)
+    grad_projected = join_heads(grads, row_count).transpose(1, 0, 2)
+    return output, grad_projected, total.astype(F32)
+
+
+def head_blocks(values, ranks):
+    return jnp.stack([values[:, h * HD : (h + 1) * HD] for h in range(ranks)])
+
+
+def _split_kernel(ranks, x_ref, tail_ref, out_ref):
+    rows = x_ref.shape[1]
+    for head in range(ranks):
+        for part in range(3):
+            block = x_ref[part, :, head * HD : (head + 1) * HD]
+            out_ref[head, part * rows : (part + 1) * rows, :] = block
+        out_ref[head, 3 * rows :, :] = tail_ref[...]
+
+
+def split_heads(x, tail, ranks):
+    vmem = pl.BlockSpec(memory_space=pltpu.VMEM)
+    return pl.pallas_call(
+        functools.partial(_split_kernel, ranks),
+        out_shape=jax.ShapeDtypeStruct((ranks, 3 * x.shape[1] + tail.shape[0], HD), BF),
+        in_specs=[vmem] * 2,
+        out_specs=vmem,
+        compiler_params=pltpu.CompilerParams(vmem_limit_bytes=24 * 1024 * 1024),
+        cost_estimate=pl.CostEstimate(flops=0, bytes_accessed=4 * x.size, transcendentals=0),
+        name="split_heads",
+    )(x, tail)
+
+
+def _join_kernel(x_ref, out_ref):
+    for head in range(x_ref.shape[0]):
+        for part in range(3):
+            out_ref[part, :, head * HD : (head + 1) * HD] = x_ref[head, part]
+
+
+def join_heads(x, rows):
+    vmem = pl.BlockSpec(memory_space=pltpu.VMEM)
+    return pl.pallas_call(
+        _join_kernel,
+        out_shape=jax.ShapeDtypeStruct((3, rows, x.shape[0] * HD), BF),
+        in_specs=[vmem],
+        out_specs=vmem,
+        compiler_params=pltpu.CompilerParams(vmem_limit_bytes=24 * 1024 * 1024),
+        cost_estimate=pl.CostEstimate(flops=0, bytes_accessed=4 * x.size, transcendentals=0),
+        name="join_heads",
+    )(x)
+
+
+def _reduce_kernel(
+    ranks, factor, sent_ref, product_ref, other_ref, out_ref, pair_out, pair_in, first_out, ring_in,
+    tp_send, tp_recv, pair_send, pair_recv, sum_send, sum_recv, all_send, all_recv, last_send, last_recv
+):
+    core, seq, tp = lax.axis_index("dp"), lax.axis_index("seq"), lax.axis_index("tp")
+    half, columns = product_ref.shape[0] // 2, product_ref.shape[1]
+    chunk, wide = half // ranks, columns // 2
+    mesh = pl.DeviceIdType.MESH
+
+    def flip(index):
+        z, x = index // 2, index % 2
+        return z + x * (ranks - 1 - 2 * z)
+
+    def unflip(place):
+        x = place // (ranks // 2)
+        return 2 * (place + x * (ranks - 1 - 2 * place)) + x
+
+    me = flip(seq)
+    ring = ({"seq": unflip((me + 1) % ranks)}, {"seq": unflip((me + ranks - 1) % ranks)})
+    partner, across = {"dp": 1 - core}, {"tp": 1 - tp}
+
+    barrier = pltpu.get_barrier_semaphore()
+    for device in (*ring, partner, across):
+        pl.semaphore_signal(barrier, inc=1, device_id=device, device_id_type=mesh)
+    pl.semaphore_wait(barrier, 4)
+
+    def send(source, target, send_sem, recv_sem, device):
+        copy = pltpu.make_async_remote_copy(
+            src_ref=source, dst_ref=target, send_sem=send_sem, recv_sem=recv_sem,
+            device_id=device, device_id_type=mesh,
+        )
+        copy.start()
+        return copy
+
+    def place(offset):
+        return (me + offset + ranks) % ranks
+
+    def chunk_rows(start, index):
+        return pl.ds(pl.multiple_of(start + index * chunk, chunk), chunk)
+
+    offsets = sorted(range(1, ranks), key=lambda o: (min(o, ranks - o), o)) + [0]
+    pair = {}
+    for slot, offset in enumerate(offsets):
+        rows = chunk_rows((1 - core) * half, place(offset))
+        pair_out[slot] = product_ref[rows, :].astype(BF)
+        pair[offset] = (
+            slot,
+            send(pair_out.at[slot], pair_in.at[slot], pair_send.at[slot], pair_recv.at[slot], partner),
+        )
+    crossing = send(sent_ref, other_ref, tp_send, tp_recv, across)
+    here = set()
+
+    def own(offset, cols):
+        offset = offset % ranks
+        slot, copy = pair[offset]
+        if offset not in here:
+            here.add(offset)
+            copy.wait_recv()
+        rows = chunk_rows(core * half, place(offset))
+        return product_ref[rows, cols] + pair_in[slot, :, cols].astype(F32)
+
+    cols = (slice(0, wide), slice(wide, columns))
+    copies = []
+    moving = [None, None]
+    for way in range(2):
+        sign = -1 if way == 0 else 1
+        first_out[way] = own(sign, cols[way]).astype(BF)
+        moving[way] = send(
+            first_out.at[way], ring_in.at[way, 0], sum_send.at[way, 0], sum_recv.at[way, 0], ring[way]
+        )
+        copies.append(moving[way])
+    for step in range(1, ranks):
+        for way in range(2):
+            sign = -1 if way == 0 else 1
+            mine = own(sign * (step + 1), cols[way])
+            moving[way].wait_recv()
+            value = mine + ring_in[way, step - 1].astype(F32)
+            if step < ranks - 1:
+                ring_in[way, step - 1] = value.astype(BF)
+                moving[way] = send(
+                    ring_in.at[way, step - 1], ring_in.at[way, step],
+                    sum_send.at[way, step], sum_recv.at[way, step], ring[way],
+                )
+                copies.append(moving[way])
+            else:
+                out_ref[chunk_rows(core * half, me), cols[way]] = (value * factor).astype(BF)
+
+    arrived = [None, None]
+    finals = []
+    for step in range(ranks):
+        for way in range(2):
+            sign = -1 if way == 0 else 1
+            if step > 0:
+                arrived[way].wait_recv()
+            view = out_ref.at[chunk_rows(core * half, place(sign * step)), cols[way]]
+            if step < ranks - 1:
+                arrived[way] = send(view, view, all_send.at[way, step], all_recv.at[way, step], ring[way])
+                copies.append(arrived[way])
+            final = send(view, view, last_send.at[way, step], last_recv.at[way, step], partner)
+            finals.append(final)
+    for copy in copies:
+        copy.wait_send()
+    for _, copy in pair.values():
+        copy.wait_send()
+    for copy in finals:
+        copy.wait()
+    crossing.wait()
+
+
+def reduce_sums(sent, product, ranks, factor):
     half, columns = product.shape[0] // 2, product.shape[1]
-    first = lax.axis_index("dp") == 0
-    pairs = [(0, 1), (1, 0)]
-    mine = jnp.where(first, product[:half], product[half:])
-    sent = jnp.where(first, product[half:], product[:half]).astype(BF)
-    mine = mine + lax.ppermute(sent, "dp", pairs).astype(F32)
-    blocks = mine.astype(BF).reshape(ranks, half // ranks, columns)
-    blocks = lax.all_to_all(blocks, "seq", split_axis=0, concat_axis=0, tiled=True)
-    total = (jnp.sum(blocks.astype(F32), axis=0) * factor).astype(BF)
-    total = lax.all_gather(total, "seq", axis=0, tiled=True)
-    other = lax.ppermute(total, "dp", pairs)
-    both = jnp.where(
-        first, jnp.concatenate([total, other]), jnp.concatenate([other, total])
-    )
-    return both.astype(F32)
+    chunk = half // ranks
+    dma = pltpu.SemaphoreType.DMA
+    vmem = pl.BlockSpec(memory_space=pltpu.VMEM)
+    return pl.pallas_call(
+        functools.partial(_reduce_kernel, ranks, factor),
+        out_shape=(
+            jax.ShapeDtypeStruct(sent.shape, BF),
+            jax.ShapeDtypeStruct(product.shape, BF),
+        ),
+        in_specs=[vmem] * 2,
+        out_specs=(vmem, vmem),
+        scratch_shapes=[
+            pltpu.VMEM((ranks, chunk, columns), BF),
+            pltpu.VMEM((ranks, chunk, columns), BF),
+            pltpu.VMEM((2, chunk, columns // 2), BF),
+            pltpu.VMEM((2, ranks - 1, chunk, columns // 2), BF),
+            dma, dma,
+            *[dma((ranks,))] * 2,
+            *[dma((2, ranks))] * 6,
+        ],
+        compiler_params=pltpu.CompilerParams(
+            collective_id=0, has_side_effects=True, vmem_limit_bytes=40 * 1024 * 1024
+        ),
+        cost_estimate=pl.CostEstimate(flops=6 * 10**10, bytes_accessed=2 * 10**7, transcendentals=0),
+        name="reduce_sums",
+    )(sent, product)
 
 
 masked_score = -1e30
@@ -402,7 +568,8 @@
         P("tp", None),
         P(("dp", "seq"), "tp"),
     )
-    whole_heads = 2048 // HD // mesh.shape["tp"] == mesh.shape["seq"]
+    sizes = mesh.shape
+    whole_heads = 2048 // HD // sizes["tp"] == sizes["seq"] and sizes["tp"] == 2 == sizes["dp"]
     return jax.shard_map(
         on_device if whole_heads else packed_on_device,
         mesh=mesh,

time: 258 us -> 201 us (0.78)
  Pallas kernels: 21 us -> 111 us
  blocking collectives: 77.4 us -> 0 us
  waiting for transfers between devices: 91 us -> 39.5 us
  between operations: 14.2 us -> 0.76 us
    pallas_call x0 -> x3, Pallas kernels: none -> 91.7 us  [the longest x1 88.6 us: reduce_sums(): pl.pallas_call(functools.partial(_reduce_kernel, ranks, factor), out_shap...]
    all_to_all x2 -> x0, blocking collectives: 77.4 us -> none  [the longest x1 52.8 us: total_over_rows(): lax.all_to_all(blocks, 'seq', split_axis=0, concat_axis=0, tiled=True)]
    ppermute x3 -> x0, waiting for transfers between devices: 17 us -> none  [the longest x1 12.9 us: project(): other = lax.ppermute(sent, 'tp', [(0, 1), (1, 0)])]
    all_to_all x3, waiting for transfers between devices: 51 us -> 37.8 us  [the longest x1 29.6 us: on_device(): exchange(split_heads(projected.transpose(1, 0, 2), tail.astype(BF), ranks))]
    all_to_all x1, waiting for transfers between devices: 11.7 us -> 0.01 us  [on_device(): grads = exchange(back)]
    all_gather x1 -> x0, waiting for transfers between devices: 11.2 us -> none  [total_over_rows(): total = lax.all_gather(total, 'seq', axis=0, tiled=True)]
    unnamed x4 -> x20, local copies, waits for them, and re-layouts: 3.45 us -> 8.43 us
    convert_element_type x6 -> x4, other arithmetic: 10.1 us -> 5.62 us  [the longest x1 4.47 us: on_device(): return (output, grad_projected, total.astype(F32))]
  transfers between devices with their start and end apart: 9 -> 5, of which waited for: 7 -> 4; matrix products, arithmetic and copies ran while one was open for 7% -> 13% of each run, Pallas kernels for 5% -> 55%
where the time goes in v2:
time: 201 us; the launch traced here: 200 us
  Pallas kernels  111 us (55%)
  waiting for transfers between devices  39.5 us (20%)
  starting transfers between devices  20.6 us (10%)
  local copies, waits for them, and re-layouts  9.93 us (5%)
  other arithmetic  9.43 us (5%)
  matrix products  8.21 us (4%)
    pallas_call x1, Pallas kernels, reduce_sums(): pl.pallas_call(functools.partial(_reduce_kernel, ranks, factor), out_shap...  88.6 us
    all_to_all x1, waiting for transfers between devices, on_device(): exchange(split_heads(projected.transpose(1, 0, 2), tail.astype(BF), ranks))  29.6 us
    pallas_call x2, Pallas kernels, attend(): pl.pallas_call(functools.partial(_attend_kernel, backward, ranks, run_cou...  19.7 us
    unnamed x20, local copies, waits for them, and re-layouts  8.43 us
    dot_general x3, matrix products, _dot(): lax.dot_general(a, b, (((ca,), (cb,)), ((), ())), preferred_element_type=...  8.21 us
    all_to_all x1, waiting for transfers between devices, on_device(): g = exchange(blocks)  6.08 us
    all_to_all x1, starting transfers between devices, on_device(): exchange(split_heads(projected.transpose(1, 0, 2), tail.astype(BF), ranks))  5.94 us
    convert_element_type x1, other arithmetic, on_device(): return (output, grad_projected, total.astype(F32))  4.47 us
  transfers between devices with their start and end apart: 5, of which 4 were waited for; matrix products, arithmetic and copies ran while one was open for 13% of the time, Pallas kernels for 55%

profile of v2, /device:TPU:0, one launch (start us, length us, event | category | flops | bytes accessed | tf_op | source)
XLA Modules:
  0.0 199.7 jit_solution(6556919696764636517)
XLA Ops:
  0.6 3.0 %collective-permute-start = (bf16[256,1024]{1,0:T(8,128)(2,1)}, bf16[256,1024]{1,0:T(8,128)(2,1)}, u32[]{:S(2)}, u32[]{:S(2)}) collective-permute-start(bf16[256,1024]{1,0:T(8,128)(2,1)} %param.9), channel_id=1, source_target_pairs={{0,1},{1,0},{2,3},{3,2},{4,5},{5,4},{6,7},{7,6},{8,9},{9,8},{10,11... | collective-permute-start | bytes 1572872 | tf_op jit(solution)/shard_map/ppermute | solution.py:163
  3.7 0.7 convert.15
  4.3 0.1 reshape.63
  4.4 0.7 convert.16
  5.1 0.1 reshape.64
  5.2 0.1 slice_reduce_fusion
  5.3 0.1 fusion.9
  5.4 1.4 copy-done
  6.8 1.4 split_heads.1
  8.3 5.9 %all-to-all-start = ((bf16[8,784,128]{2,1,0:T(8,128)(2,1)}), bf16[8,784,128]{2,1,0:T(8,128)(2,1)S(1)}, u32[]{:S(2)}, u32[]{:S(2)}) async-start(bf16[8,784,128]{2,1,0:T(8,128)(2,1)} %split_heads.1), calls=%async_computation | async-start | bytes 3211264 | tf_op jit(solution)/shard_map/all_to_all | solution.py:188
  14.2 1.7 collective-permute-done
  15.9 0.0 copy-done.2
  15.9 1.6 maximum_select_fusion
  17.5 3.5 %convolution_convert_fusion = bf16[256,1024]{1,0:T(8,128)(2,1)S(1)} fusion(bf16[256,2048]{1,0:T(8,128)(2,1)S(1)} %maximum_select_fusion, bf16[1024,2048]{1,0:T(8,128)(2,1)} %param.8), kind=kOutput, calls=%fused_computation | convolution fusion | flops 1074003968 | bytes 5767168 | tf_op jit(solution)/shard_map/dot_general | solution.py:18
  21.2 0.0 copy-start.1
  21.2 0.8 copy-done.1
  22.0 29.6 %all-to-all-done.refs_0_ = bf16[8,784,128]{2,1,0:T(8,128)(2,1)S(1)} async-done(((bf16[8,784,128]{2,1,0:T(8,128)(2,1)}), bf16[8,784,128]{2,1,0:T(8,128)(2,1)S(1)}, u32[]{:S(2)}, u32[]{:S(2)}) %all-to-all-start) | async-done | bytes 1605664 | tf_op jit(solution)/shard_map/all_to_all | solution.py:188
  51.6 3.6 %all-to-all-start.2 = ((bf16[8,256,128]{2,1,0:T(8,128)(2,1)}), bf16[8,256,128]{2,1,0:T(8,128)(2,1)S(1)}, u32[]{:S(2)}, u32[]{:S(2)}) async-start(bf16[8,256,128]{2,1,0:T(8,128)(2,1)} %copy-done.1), calls=%async_computation.2 | async-start | bytes 1048576 | tf_op jit(solution)/shard_map/all_to_all | solution.py:198
  55.3 0.1 slice_add_fusion
  55.3 0.1 add.19
  55.4 0.1 eq.37
  55.5 0.2 convert_reduce_fusion
  55.7 0.3 select_reduce_fusion
  56.1 0.1 sub.7.gathers
  56.2 0.1 reshape.65.order
  56.3 0.1 convert_reduce_fusion.1.counts
  56.4 7.5 %attend.1.refs_1_ = bf16[8,256,128]{2,1,0:T(8,128)(2,1)} custom-call(s32[8]{0:T(128)S(1)} %convert_reduce_fusion.1.counts, s32[64]{0:T(128)S(1)} %reshape.65.order, s32[64]{0:T(128)S(1)} %sub.7.gathers, bf16[8,784,128]{2,1,0:T(8,128)(2,1)S(1)} %all-to-all-done.refs_0_), custom_call_target="tpu_custom_call" | custom-call | flops 200000000 | bytes 3000000 | tf_op jit(solution)/shard_map/attend/pallas_call | solution.py:128
  63.9 6.1 %all-to-all-done.2.refs_2_ = bf16[8,256,128]{2,1,0:T(8,128)(2,1)S(1)} async-done(((bf16[8,256,128]{2,1,0:T(8,128)(2,1)}), bf16[8,256,128]{2,1,0:T(8,128)(2,1)S(1)}, u32[]{:S(2)}, u32[]{:S(2)}) %all-to-all-start.2) | async-done | bytes 524320 | tf_op jit(solution)/shard_map/all_to_all | solution.py:198
  69.9 4.1 %all-to-all-start.1 = ((bf16[8,256,128]{2,1,0:T(8,128)(2,1)}), bf16[8,256,128]{2,1,0:T(8,128)(2,1)}, u32[]{:S(2)}, u32[]{:S(2)}) async-start(bf16[8,256,128]{2,1,0:T(8,128)(2,1)} %attend.1.refs_1_), calls=%async_computation.1 | async-start | bytes 1048576 | tf_op jit(solution)/shard_map/all_to_all | solution.py:201
  74.1 12.2 %attend_back.1 = bf16[8,3,256,128]{3,2,1,0:T(8,128)(2,1)} custom-call(s32[8]{0:T(128)S(1)} %convert_reduce_fusion.1.counts, s32[64]{0:T(128)S(1)} %reshape.65.order, s32[64]{0:T(128)S(1)} %sub.7.gathers, bf16[8,784,128]{2,1,0:T(8,128)(2,1)S(1)} %all-to-all-done.refs_0_, bf16[8,256,128]{2,1,0:T(8,128)(2,1)} %attend.1.refs_1_, ...), custom_call_target="tpu_custom_call" | custom-call | flops 600000000 | bytes 3000000 | tf_op jit(solution)/shard_map/attend_back/pallas_call | solution.py:128
  86.3 2.1 %all-to-all-done.1 = bf16[8,256,128]{2,1,0:T(8,128)(2,1)} async-done(((bf16[8,256,128]{2,1,0:T(8,128)(2,1)}), bf16[8,256,128]{2,1,0:T(8,128)(2,1)}, u32[]{:S(2)}, u32[]{:S(2)}) %all-to-all-start.1) | async-done | bytes 524320 | tf_op jit(solution)/shard_map/all_to_all | solution.py:201
  88.4 3.8 %all-to-all-start.3 = ((bf16[8,3,256,128]{3,2,1,0:T(8,128)(2,1)}), bf16[8,3,256,128]{3,2,1,0:T(8,128)(2,1)S(1)}, u32[]{:S(2)}, u32[]{:S(2)}) async-start(bf16[8,3,256,128]{3,2,1,0:T(8,128)(2,1)} %attend_back.1), calls=%async_computation.3 | async-start | bytes 3145728 | tf_op jit(solution)/shard_map/all_to_all | solution.py:204
  92.2 0.9 bitcast_dynamic-update-slice_fusion.7
  93.0 0.9 bitcast_dynamic-update-slice_fusion.6
  93.9 0.9 bitcast_dynamic-update-slice_fusion.5
  94.8 0.9 bitcast_dynamic-update-slice_fusion.4
  95.6 0.9 bitcast_dynamic-update-slice_fusion.3
  96.5 0.9 bitcast_dynamic-update-slice_fusion.2
  97.4 0.9 bitcast_dynamic-update-slice_fusion.1
  98.2 0.9 bitcast_dynamic-update-slice_fusion
  99.1 3.4 %fusion.10 = f32[256,2048]{1,0:T(8,128)S(1)} fusion(bf16[256,1024]{1,0:T(8,128)(2,1)S(1)} %bitcast_dynamic-update-slice_fusion, bf16[1024,2048]{1,0:T(8,128)(2,1)} %param.8), kind=kOutput, calls=%fused_computation.44 | convolution fusion | flops 1073741824 | bytes 6815744 | tf_op jit(solution)/shard_map/dot_general | solution.py:18
  102.5 0.1 select_convert_fusion.sent_ref
  102.6 1.3 fusion.11.product_ref
  103.9 88.6 %reduce_sums.1 = (bf16[256,1024]{1,0:T(8,128)(2,1)S(1)}, bf16[1024,2048]{1,0:T(8,128)(2,1)S(1)}) custom-call(bf16[256,1024]{1,0:T(8,128)(2,1)S(1)} %select_convert_fusion.sent_ref, f32[1024,2048]{1,0:T(8,128)S(1)} %fusion.11.product_ref), custom_call_target="tpu_custom_call" | custom-call | flops 60000002048 | bytes 20000000 | tf_op jit(solution)/shard_map/reduce_sums/pallas_call | solution.py:379
  192.6 4.5 %convert_element_type.36 = f32[1024,2048]{1,0:T(8,128)} convert(bf16[1024,2048]{1,0:T(8,128)(2,1)S(1)} %get-tuple-element.16) | non-fusion elementwise | flops 2097152 | bytes 12582912 | tf_op jit(solution)/shard_map/convert_element_type | solution.py:217
  197.0 1.1 add_convert_fusion
  198.1 0.0 all-to-all-done.3.x_ref
  198.1 1.6 join_heads.1
  (15 shorter events, 0.3 us)
Async XLA Ops:
  0.6 15.3 %collective-permute-start = (bf16[256,1024]{1,0:T(8,128)(2,1)}, bf16[256,1024]{1,0:T(8,128)(2,1)}, u32[]{:S(2)}, u32[]{:S(2)}) collective-permute-start(bf16[256,1024]{1,0:T(8,128)(2,1)} %param.9), channel_id=1, source_target_pairs={{0,1},{1,0},{2,3},{3,2},{4,5},{5,4},{6,7},{7,6},{8,9},{9,8},{10,11... | collective-permute-start | bytes 1572872 | tf_op jit(solution)/shard_map/ppermute | solution.py:163
  5.4 1.4 copy-start
  8.3 7.6 %copy-start.2 = (bf16[256,1024]{1,0:T(8,128)(2,1)S(1)}, bf16[256,1024]{1,0:T(8,128)(2,1)}, u32[]{:S(2)}) copy-start(bf16[256,1024]{1,0:T(8,128)(2,1)} %param.9) | copy-start | bytes 1572868
  8.3 43.4 %all-to-all-start = ((bf16[8,784,128]{2,1,0:T(8,128)(2,1)}), bf16[8,784,128]{2,1,0:T(8,128)(2,1)S(1)}, u32[]{:S(2)}, u32[]{:S(2)}) async-start(bf16[8,784,128]{2,1,0:T(8,128)(2,1)} %split_heads.1), calls=%async_computation | async-start | bytes 3211264 | tf_op jit(solution)/shard_map/all_to_all | solution.py:188
  21.2 0.8 copy-start.1
  51.6 18.3 %all-to-all-start.2 = ((bf16[8,256,128]{2,1,0:T(8,128)(2,1)}), bf16[8,256,128]{2,1,0:T(8,128)(2,1)S(1)}, u32[]{:S(2)}, u32[]{:S(2)}) async-start(bf16[8,256,128]{2,1,0:T(8,128)(2,1)} %copy-done.1), calls=%async_computation.2 | async-start | bytes 1048576 | tf_op jit(solution)/shard_map/all_to_all | solution.py:198
  69.9 18.4 %all-to-all-start.1 = ((bf16[8,256,128]{2,1,0:T(8,128)(2,1)}), bf16[8,256,128]{2,1,0:T(8,128)(2,1)}, u32[]{:S(2)}, u32[]{:S(2)}) async-start(bf16[8,256,128]{2,1,0:T(8,128)(2,1)} %attend.1.refs_1_), calls=%async_computation.1 | async-start | bytes 1048576 | tf_op jit(solution)/shard_map/all_to_all | solution.py:201
  88.4 109.7 %all-to-all-start.3 = ((bf16[8,3,256,128]{3,2,1,0:T(8,128)(2,1)}), bf16[8,3,256,128]{3,2,1,0:T(8,128)(2,1)S(1)}, u32[]{:S(2)}, u32[]{:S(2)}) async-start(bf16[8,3,256,128]{3,2,1,0:T(8,128)(2,1)} %attend_back.1), calls=%async_computation.3 | async-start | bytes 3145728 | tf_op jit(solution)/shard_map/all_to_all | solution.py:204

commit v3 on v2

--- a/solution.py
+++ b/solution.py
@@ -202,7 +202,7 @@
     back = attend(True, ranks, run_count, run_rows, tables, x, attended, g)
     attended_rows, back = lax.optimization_barrier((attended_rows, back))
     grads = exchange(back)
-    attended_rows = jnp.concatenate([attended_rows[h] for h in range(ranks)], axis=1)
+    attended_rows = attended_rows.transpose(1, 0, 2).reshape(row_count, width)
 
     partial_terms = _dot(attended_rows, out_weight, 1, 0)
     product = _dot(attended_rows, columns, 0, 0)

time: 201 us -> 202 us (level)
  Pallas kernels: 111 us -> 118 us
  local copies, waits for them, and re-layouts: 9.93 us -> 4.31 us
    pallas_call x1, Pallas kernels: 88.6 us -> 95.4 us  [reduce_sums(): pl.pallas_call(functools.partial(_reduce_kernel, ranks, factor), out_shap...]
    unnamed x20 -> x13, local copies, waits for them, and re-layouts: 8.43 us -> 2.42 us
  transfers between devices with their start and end apart: 5 -> 5, of which waited for: 4 -> 4; matrix products, arithmetic and copies ran while one was open for 13% -> 9% of each run, Pallas kernels for 55% -> 58%
where the time goes in v3:
time: 202 us; the launch traced here: 201 us
  Pallas kernels  118 us (58%)
  waiting for transfers between devices  39.2 us (19%)
  starting transfers between devices  20.7 us (10%)
  other arithmetic  9.43 us (5%)
  matrix products  8.18 us (4%)
  local copies, waits for them, and re-layouts  4.31 us (2%)
    pallas_call x1, Pallas kernels, reduce_sums(): pl.pallas_call(functools.partial(_reduce_kernel, ranks, factor), out_shap...  95.4 us
    all_to_all x1, waiting for transfers between devices, on_device(): exchange(split_heads(projected.transpose(1, 0, 2), tail.astype(BF), ranks))  29.6 us
    pallas_call x2, Pallas kernels, attend(): pl.pallas_call(functools.partial(_attend_kernel, backward, ranks, run_cou...  19.9 us
    dot_general x3, matrix products, _dot(): lax.dot_general(a, b, (((ca,), (cb,)), ((), ())), preferred_element_type=...  8.18 us
    all_to_all x1, waiting for transfers between devices, on_device(): g = exchange(blocks)  5.96 us
    all_to_all x1, starting transfers between devices, on_device(): exchange(split_heads(projected.transpose(1, 0, 2), tail.astype(BF), ranks))  5.94 us
    convert_element_type x1, other arithmetic, on_device(): return (output, grad_projected, total.astype(F32))  4.47 us
    all_to_all x1, starting transfers between devices, on_device(): attended_rows = exchange(attended)  4.14 us
  transfers between devices with their start and end apart: 5, of which 4 were waited for; matrix products, arithmetic and copies ran while one was open for 9% of the time, Pallas kernels for 58%

profile of v3, /device:TPU:0, one launch (start us, length us, event | category | flops | bytes accessed | tf_op | source)
XLA Modules:
  0.0 200.9 jit_solution(10624419141406851755)
XLA Ops:
  0.6 3.0 %collective-permute-start = (bf16[256,1024]{1,0:T(8,128)(2,1)}, bf16[256,1024]{1,0:T(8,128)(2,1)}, u32[]{:S(2)}, u32[]{:S(2)}) collective-permute-start(bf16[256,1024]{1,0:T(8,128)(2,1)} %param.9), channel_id=1, source_target_pairs={{0,1},{1,0},{2,3},{3,2},{4,5},{5,4},{6,7},{7,6},{8,9},{9,8},{10,11... | collective-permute-start | bytes 1572872 | tf_op jit(solution)/shard_map/ppermute | solution.py:163
  3.7 0.7 convert.15
  4.3 0.1 reshape.66
  4.4 0.7 convert.16
  5.1 0.1 reshape.67
  5.2 0.1 slice_reduce_fusion
  5.3 0.1 fusion.9
  5.4 0.0 copy-start
  5.4 1.4 copy-done
  6.8 1.4 split_heads.1
  8.3 0.0 copy-start.2
  8.3 5.9 %all-to-all-start = ((bf16[8,784,128]{2,1,0:T(8,128)(2,1)}), bf16[8,784,128]{2,1,0:T(8,128)(2,1)S(1)}, u32[]{:S(2)}, u32[]{:S(2)}) async-start(bf16[8,784,128]{2,1,0:T(8,128)(2,1)} %split_heads.1), calls=%async_computation | async-start | bytes 3211264 | tf_op jit(solution)/shard_map/all_to_all | solution.py:188
  14.2 1.7 collective-permute-done
  15.9 0.0 copy-done.2
  15.9 1.6 maximum_select_fusion
  17.5 3.5 %convolution_convert_fusion = bf16[256,1024]{1,0:T(8,128)(2,1)S(1)} fusion(bf16[256,2048]{1,0:T(8,128)(2,1)S(1)} %maximum_select_fusion, bf16[1024,2048]{1,0:T(8,128)(2,1)} %param.8), kind=kOutput, calls=%fused_computation | convolution fusion | flops 1074003968 | bytes 5767168 | tf_op jit(solution)/shard_map/dot_general | solution.py:18
  21.2 0.0 copy-start.1
  21.2 0.8 copy-done.1
  22.0 29.6 %all-to-all-done.refs_0_ = bf16[8,784,128]{2,1,0:T(8,128)(2,1)S(1)} async-done(((bf16[8,784,128]{2,1,0:T(8,128)(2,1)}), bf16[8,784,128]{2,1,0:T(8,128)(2,1)S(1)}, u32[]{:S(2)}, u32[]{:S(2)}) %all-to-all-start) | async-done | bytes 1605664 | tf_op jit(solution)/shard_map/all_to_all | solution.py:188
  51.6 3.6 %all-to-all-start.2 = ((bf16[8,256,128]{2,1,0:T(8,128)(2,1)}), bf16[8,256,128]{2,1,0:T(8,128)(2,1)S(1)}, u32[]{:S(2)}, u32[]{:S(2)}) async-start(bf16[8,256,128]{2,1,0:T(8,128)(2,1)} %copy-done.1), calls=%async_computation.2 | async-start | bytes 1048576 | tf_op jit(solution)/shard_map/all_to_all | solution.py:198
  55.3 0.1 slice_add_fusion
  55.3 0.1 add.19
  55.4 0.1 eq.37
  55.5 0.2 convert_reduce_fusion
  55.7 0.3 select_reduce_fusion
  56.1 0.1 sub.7.gathers
  56.2 0.1 reshape.68.order
  56.3 0.1 convert_reduce_fusion.1.counts
  56.4 7.6 %attend.1.refs_1_ = bf16[8,256,128]{2,1,0:T(8,128)(2,1)} custom-call(s32[8]{0:T(128)S(1)} %convert_reduce_fusion.1.counts, s32[64]{0:T(128)S(1)} %reshape.68.order, s32[64]{0:T(128)S(1)} %sub.7.gathers, bf16[8,784,128]{2,1,0:T(8,128)(2,1)S(1)} %all-to-all-done.refs_0_), custom_call_target="tpu_custom_call" | custom-call | flops 200000000 | bytes 3000000 | tf_op jit(solution)/shard_map/attend/pallas_call | solution.py:128
  64.0 6.0 %all-to-all-done.2.refs_2_ = bf16[8,256,128]{2,1,0:T(8,128)(2,1)S(1)} async-done(((bf16[8,256,128]{2,1,0:T(8,128)(2,1)}), bf16[8,256,128]{2,1,0:T(8,128)(2,1)S(1)}, u32[]{:S(2)}, u32[]{:S(2)}) %all-to-all-start.2) | async-done | bytes 524320 | tf_op jit(solution)/shard_map/all_to_all | solution.py:198
  69.9 4.1 %all-to-all-start.1 = ((bf16[8,256,128]{2,1,0:T(8,128)(2,1)}), bf16[8,256,128]{2,1,0:T(8,128)(2,1)}, u32[]{:S(2)}, u32[]{:S(2)}) async-start(bf16[8,256,128]{2,1,0:T(8,128)(2,1)} %attend.1.refs_1_), calls=%async_computation.1 | async-start | bytes 1048576 | tf_op jit(solution)/shard_map/all_to_all | solution.py:201
  74.1 12.3 %attend_back.1 = bf16[8,3,256,128]{3,2,1,0:T(8,128)(2,1)} custom-call(s32[8]{0:T(128)S(1)} %convert_reduce_fusion.1.counts, s32[64]{0:T(128)S(1)} %reshape.68.order, s32[64]{0:T(128)S(1)} %sub.7.gathers, bf16[8,784,128]{2,1,0:T(8,128)(2,1)S(1)} %all-to-all-done.refs_0_, bf16[8,256,128]{2,1,0:T(8,128)(2,1)} %attend.1.refs_1_, ...), custom_call_target="tpu_custom_call" | custom-call | flops 600000000 | bytes 3000000 | tf_op jit(solution)/shard_map/attend_back/pallas_call | solution.py:128
  86.4 2.0 all-to-all-done.1
  88.4 1.2 copy.10
  89.6 3.9 %all-to-all-start.3 = ((bf16[8,3,256,128]{3,2,1,0:T(8,128)(2,1)}), bf16[8,3,256,128]{3,2,1,0:T(8,128)(2,1)S(1)}, u32[]{:S(2)}, u32[]{:S(2)}) async-start(bf16[8,3,256,128]{3,2,1,0:T(8,128)(2,1)} %attend_back.1), calls=%async_computation.3 | async-start | bytes 3145728 | tf_op jit(solution)/shard_map/all_to_all | solution.py:204
  93.6 3.5 %fusion.10 = f32[256,2048]{1,0:T(8,128)S(1)} fusion(bf16[256,1024]{0,1:T(8,128)(2,1)S(1)} %bitcast.44, bf16[1024,2048]{1,0:T(8,128)(2,1)} %param.8), kind=kOutput, calls=%fused_computation.36 | convolution fusion | flops 1073741824 | bytes 6815744 | tf_op jit(solution)/shard_map/dot_general | solution.py:18
  97.0 0.1 select_convert_fusion.sent_ref
  97.1 1.3 fusion.11.product_ref
  98.4 95.4 %reduce_sums.1 = (bf16[256,1024]{1,0:T(8,128)(2,1)S(1)}, bf16[1024,2048]{1,0:T(8,128)(2,1)S(1)}) custom-call(bf16[256,1024]{1,0:T(8,128)(2,1)S(1)} %select_convert_fusion.sent_ref, f32[1024,2048]{1,0:T(8,128)S(1)} %fusion.11.product_ref), custom_call_target="tpu_custom_call" | custom-call | flops 60000002048 | bytes 20000000 | tf_op jit(solution)/shard_map/reduce_sums/pallas_call | solution.py:379
  193.7 4.5 %convert_element_type.36 = f32[1024,2048]{1,0:T(8,128)} convert(bf16[1024,2048]{1,0:T(8,128)(2,1)S(1)} %get-tuple-element.16) | non-fusion elementwise | flops 2097152 | bytes 12582912 | tf_op jit(solution)/shard_map/convert_element_type | solution.py:217
  198.2 1.1 add_convert_fusion
  199.3 0.0 all-to-all-done.3.x_ref
  199.3 1.6 join_heads.1
  (13 shorter events, 0.3 us)
Async XLA Ops:
  0.6 15.3 %collective-permute-start = (bf16[256,1024]{1,0:T(8,128)(2,1)}, bf16[256,1024]{1,0:T(8,128)(2,1)}, u32[]{:S(2)}, u32[]{:S(2)}) collective-permute-start(bf16[256,1024]{1,0:T(8,128)(2,1)} %param.9), channel_id=1, source_target_pairs={{0,1},{1,0},{2,3},{3,2},{4,5},{5,4},{6,7},{7,6},{8,9},{9,8},{10,11... | collective-permute-start | bytes 1572872 | tf_op jit(solution)/shard_map/ppermute | solution.py:163
  5.4 1.4 copy-start
  8.3 7.6 %copy-start.2 = (bf16[256,1024]{1,0:T(8,128)(2,1)S(1)}, bf16[256,1024]{1,0:T(8,128)(2,1)}, u32[]{:S(2)}) copy-start(bf16[256,1024]{1,0:T(8,128)(2,1)} %param.9) | copy-start | bytes 1572868
  8.3 43.4 %all-to-all-start = ((bf16[8,784,128]{2,1,0:T(8,128)(2,1)}), bf16[8,784,128]{2,1,0:T(8,128)(2,1)S(1)}, u32[]{:S(2)}, u32[]{:S(2)}) async-start(bf16[8,784,128]{2,1,0:T(8,128)(2,1)} %split_heads.1), calls=%async_computation | async-start | bytes 3211264 | tf_op jit(solution)/shard_map/all_to_all | solution.py:188
  21.2 0.8 copy-start.1
  51.6 18.3 %all-to-all-start.2 = ((bf16[8,256,128]{2,1,0:T(8,128)(2,1)}), bf16[8,256,128]{2,1,0:T(8,128)(2,1)S(1)}, u32[]{:S(2)}, u32[]{:S(2)}) async-start(bf16[8,256,128]{2,1,0:T(8,128)(2,1)} %copy-done.1), calls=%async_computation.2 | async-start | bytes 1048576 | tf_op jit(solution)/shard_map/all_to_all | solution.py:198
  69.9 18.4 %all-to-all-start.1 = ((bf16[8,256,128]{2,1,0:T(8,128)(2,1)}), bf16[8,256,128]{2,1,0:T(8,128)(2,1)}, u32[]{:S(2)}, u32[]{:S(2)}) async-start(bf16[8,256,128]{2,1,0:T(8,128)(2,1)} %attend.1.refs_1_), calls=%async_computation.1 | async-start | bytes 1048576 | tf_op jit(solution)/shard_map/all_to_all | solution.py:201
  89.6 109.6 %all-to-all-start.3 = ((bf16[8,3,256,128]{3,2,1,0:T(8,128)(2,1)}), bf16[8,3,256,128]{3,2,1,0:T(8,128)(2,1)S(1)}, u32[]{:S(2)}, u32[]{:S(2)}) async-start(bf16[8,3,256,128]{3,2,1,0:T(8,128)(2,1)} %attend_back.1), calls=%async_computation.3 | async-start | bytes 3145728 | tf_op jit(solution)/shard_map/all_to_all | solution.py:204
